TPU v7x, 32 devices: a whole 2x2x4 slice. The times are simulated.
32 devices in a mesh: seq: 8 (over z, x), diag: 4 (over y, core).
Axes of the slice: x: 2, y: 2, z: 4, core: 2. Of those that a mesh axis runs over, the one named last changes fastest.
Arguments:
- seq_feat: bfloat16 [512, 128], P('seq'), may hold values from -6 to 6
- conv1_weight: bfloat16 [2, 3, 128, 128], replicated, may hold values from -0.3125 to 0.3125
- conv2_kernel_weight: bfloat16 [3, 3, 128, 128], replicated, may hold values from -0.1875 to 0.1875
- dilations: int32 [3], replicated, may hold values from 1 to 8, as said below
- block_mask: int32 [8, 8], P('seq', 'diag'), may hold values 0 or 1
- band_grad: bfloat16 [512, 512, 128], P('seq', 'diag'), may hold values from -0.5 to 0.5
Outputs:
- band_out: bfloat16 [512, 512, 128], P('seq', 'diag')
- seq_grad: float32 [512, 128], P('seq')
- conv1_grad: float32 [2, 3, 128, 128], replicated
- conv2_grad: float32 [3, 3, 128, 128], replicated
Inputs may be any that keep to these rules, and one draw needn't show every extreme that they name: `dilations`: one entry equals 8.
All inputs are finite; a program needn't handle non-finite values. No bound on the sum of `block_mask` on one device may be relied on, other than what follows from the above.
Results may differ from a plain program's by a relative error of at most 0.014.
Values may be sent and summed in bfloat16 or wider, within the bound.
A program may use at most 128 MiB of HBM per device.

v0:
```python
import functools
import math

import jax
import jax.numpy as jnp
from jax import lax
from jax.experimental import pallas as pl
from jax.experimental.pallas import tpu as pltpu
from jax.sharding import PartitionSpec as P

BLOCK = 64
HALO = 8
LINE_LAYERS = 2
HOFF = 16
MESH = pl.DeviceIdType.MESH

root_half = 0.7071067811865476
inv_root_two_pi = 0.3989422804014327

F32 = jnp.float32
BF16 = jnp.bfloat16


def rounded(x):
    return x.astype(BF16).astype(F32)


def gelu_pair(v):
    half = 0.5 * (1.0 + lax.erf(v * root_half))
    return v * half, half


def slope_from(v, half):
    return half + v * jnp.exp(-0.5 * v * v) * inv_root_two_pi


def dot(a, b, dims=((1,), (0,))):
    return lax.dot_general(a, b, (dims, ((), ())), preferred_element_type=F32)


def owners_for(units, devices):
    return max(n for n in range(1, devices + 1) if units % n == 0)


def kernel(
    S, D, R, B, C, NOWN,
    feat_ref, w1_ref, w2_ref, dil_ref, mask_ref, grad_ref,
    out_ref, seqg_ref, c1_ref, c2_ref,
    feat_all, hid, h1, acts, maskt, mrow, wide, p3, g3, slope, bandin, w2t,
    top, bottom, left, right, corner,
    wg, wsend, wrecv, wsum, wall, rowpart, colpart, gslots, gmine, gall, gpad,
    s_feat, r_feat, s_halo, r_halo, s_mask, r_mask, s_ws, r_ws, s_wa, r_wa,
    s_g, r_g, s_ga, r_ga,
):
    N = R * S
    W = B * D
    NDEV = S * D
    PIECE = 9 * C // NOWN
    RATIO = B // R
    Q = R // D
    s = lax.axis_index("seq")
    d = lax.axis_index("diag")
    me = s * D + d
    row0 = s * R
    d0 = d * B
    e2 = dil_ref[LINE_LAYERS]

    def device(index):
        return (index // D, index % D)

    def copy(src, dst, ss, rs, dev):
        return pltpu.make_async_remote_copy(
            src_ref=src, dst_ref=dst, send_sem=ss, recv_sem=rs,
            device_id=dev, device_id_type=MESH,
        )

    for k in range(2):
        value = mask_ref[0, k].astype(F32)
        maskt[1, 1, 8 * k : 8 * k + 8, :] = jnp.full((8, C), 1.0, F32) * value

    barrier = pltpu.get_barrier_semaphore()

    @pl.loop(1, NDEV)
    def _(step):
        pl.semaphore_signal(
            barrier, inc=1, device_id=device(lax.rem(me + step, NDEV)), device_id_type=MESH
        )

    pl.semaphore_wait(barrier, NDEV - 1)

    def feat_copy(other):
        return copy(
            feat_ref, feat_all.at[pl.ds(pl.multiple_of(row0, R), R)],
            s_feat.at[other], r_feat.at[s], (other, d),
        )

    @pl.loop(1, S)
    def _(step):
        feat_copy(lax.rem(s + step, S)).start()

    neighbours = [(a, b) for a in (-1, 0, 1) for b in (-1, 0, 1) if (a, b) != (0, 0)]

    def exists(a, b):
        return (s + a >= 0) & (s + a < S) & (d + b >= 0) & (d + b < D)

    def mask_copy(a, b):
        return copy(
            maskt.at[1, 1], maskt.at[1 - a, 1 - b],
            s_mask.at[1 + a, 1 + b], r_mask.at[1 - a, 1 - b], (s + a, d + b),
        )

    def halo_slot(a, b):
        if b == 0:
            return top if a < 0 else bottom
        if a == 0:
            return left if b < 0 else right
        return corner.at[(1 + a) // 2, (1 + b) // 2]

    def halo_copy(a, b):
        rows = {-1: pl.ds(0, HALO), 0: pl.ds(0, R), 1: pl.ds(R - HALO, HALO)}[a]
        cols = {-1: pl.ds(0, 16), 0: pl.ds(0, B), 1: pl.ds(B - 16, 16)}[b]
        return copy(
            grad_ref.at[rows, cols], halo_slot(-a, -b),
            s_halo.at[1 + a, 1 + b], r_halo.at[1 - a, 1 - b], (s + a, d + b),
        )

    for a, b in neighbours:
        @pl.when(exists(a, b))
        def _():
            mask_copy(a, b).start()

    for a, b in neighbours:
        @pl.when(exists(a, b))
        def _():
            halo_copy(a, b).start()

        @pl.when(jnp.logical_not(exists(a, b)))
        def _():
            maskt[1 + a, 1 + b] = jnp.zeros((16, C), F32)
            slot = halo_slot(a, b)
            slot[...] = jnp.zeros(slot.shape, BF16)

    feat_all[pl.ds(pl.multiple_of(row0, R), R), :] = feat_ref[...]
    hid[0:HOFF, :] = jnp.zeros((HOFF, C), F32)
    hid[HOFF + N :, :] = jnp.zeros((hid.shape[0] - HOFF - N, C), F32)
    for layer in range(LINE_LAYERS):
        acts[layer, 0:HALO, :] = jnp.zeros((HALO, C), F32)
        acts[layer, HALO + N :, :] = jnp.zeros((HALO, C), F32)
    gpad[0:HALO, :] = jnp.zeros((HALO, C), F32)
    gpad[HALO + N :, :] = jnp.zeros((HALO, C), F32)
    for a in range(3):
        for b in range(3):
            w2t[a, b * C : (b + 1) * C, :] = w2_ref[a, b].astype(F32).T.astype(BF16)
    wg[...] = jnp.zeros(wg.shape, F32)
    colpart[...] = jnp.zeros(colpart.shape, F32)

    @pl.loop(1, S)
    def _(step):
        other = lax.rem(s + step, S)
        copy(
            feat_ref, feat_all.at[pl.ds(pl.multiple_of(other * R, R), R)],
            s_feat.at[other], r_feat.at[other], (other, d),
        ).wait_recv()

    CH = min(N, 512)
    for layer in range(LINE_LAYERS):
        e = dil_ref[layer]
        for first in range(0, N, CH):
            if layer == 0:
                h = feat_all[first : first + CH, :].astype(F32)
            else:
                h = h1[first : first + CH, :]
            acts[layer, HALO + first : HALO + first + CH, :] = rounded(gelu_pair(h)[0])
        for first in range(0, N, CH):
            taps = [
                acts[layer, pl.ds(HALO + first + (t - 1) * e, CH), :].astype(BF16)
                for t in range(3)
            ]
            total = dot(taps[0], w1_ref[layer, 0])
            total = total + dot(taps[1], w1_ref[layer, 1])
            total = total + dot(taps[2], w1_ref[layer, 2])
            if layer == 0:
                h1[first : first + CH, :] = rounded(
                    feat_all[first : first + CH, :].astype(F32) + total
                )
            else:
                hid[HOFF + first : HOFF + first + CH, :] = rounded(
                    h1[first : first + CH, :] + total
                )

    for a, b in neighbours:
        @pl.when(exists(a, b))
        def _():
            copy(
                maskt.at[1, 1], maskt.at[1 + a, 1 + b],
                s_mask.at[1 + a, 1 + b], r_mask.at[1 + a, 1 + b], (s + a, d + b),
            ).wait_recv()

    for a in range(3):
        mrow[a, 0:8, :] = maskt[a, 0, 8:16, :]
        mrow[a, 8 : 8 + B // 2, :] = jnp.broadcast_to(maskt[a, 1, 0:1, :], (B // 2, C))
        mrow[a, 8 + B // 2 : 8 + B, :] = jnp.broadcast_to(maskt[a, 1, 8:9, :], (B // 2, C))
        mrow[a, 8 + B : 16 + B, :] = maskt[a, 2, 0:8, :]

    WIDE = B + 2 * HALO

    def band_row(li, kind):
        start = HOFF + row0 - HALO + li
        own = hid[pl.ds(start, 1), :]
        partner = hid[pl.ds(start + d0 - HALO, WIDE), :]
        return rounded(mrow[kind] * 0.5 * (own + partner))

    def spread(target, li, direction):
        for tap in range(3):
            piece = wide[li, pl.ds(HALO + direction * (tap - 1) * e2, B), :]
            target[li, :, tap * C : (tap + 1) * C] = piece.astype(BF16)

    def inner_row(li):
        v = band_row(li, 1)
        value, half = gelu_pair(v)
        wide[li] = rounded(value)
        mid = slice(HALO, HALO + B)
        slope[li - HALO] = slope_from(v[mid], half[mid])
        bandin[li - HALO] = v[mid].astype(BF16)
        spread(p3, li, 1)

    pl.loop(HALO, HALO + R)(inner_row)

    @pl.loop(0, 2 * HALO)
    def _(index):
        low = (index < HALO).astype(jnp.int32)
        li = index + (1 - low) * R
        wide[li] = rounded(gelu_pair(band_row(li, 2 * (1 - low)))[0])
        spread(p3, li, 1)

    for a, b in neighbours:
        @pl.when(exists(a, b))
        def _():
            copy(
                halo_slot(a, b), halo_slot(a, b),
                s_halo.at[1 + a, 1 + b], r_halo.at[1 + a, 1 + b], (s + a, d + b),
            ).wait_recv()

    def gm_row(li, kind, lo, mid, hi):
        wide[li, 0:HALO, :] = mrow[kind, 0:HALO, :] * lo.astype(F32)[8:16]
        wide[li, HALO : HALO + B, :] = mrow[kind, HALO : HALO + B, :] * mid.astype(F32)
        wide[li, HALO + B :, :] = mrow[kind, HALO + B :, :] * hi.astype(F32)[0:8]
        spread(g3, li, -1)

    @pl.loop(0, R)
    def _(i):
        gm_row(i + HALO, 1, left[i], grad_ref[i], right[i])

    @pl.loop(0, HALO)
    def _(i):
        gm_row(i, 0, corner[0, 0, i], top[i], corner[0, 1, i])
        gm_row(i + HALO + R, 2, corner[1, 0, i], bottom[i], corner[1, 1, i])

    KR = 8

    @pl.loop(0, R // KR)
    def _(step):
        i0 = HALO + step * KR
        gm = g3[pl.ds(i0, KR), :, C : 2 * C].reshape(KR * B, C)
        for a in range(3):
            pa = p3[pl.ds(i0 + (a - 1) * e2, KR)].reshape(KR * B, 3 * C)
            wg[a] += dot(gm, pa, ((0,), (0,)))

    for a in range(3):
        for b in range(3):
            wsend[(3 * a + b) * C : (3 * a + b + 1) * C, :] = (
                wg[a, :, b * C : (b + 1) * C].T.astype(BF16)
            )

    def piece_at(owner):
        return pl.ds(pl.multiple_of(owner * PIECE, 16), PIECE)

    def ws_copy(owner, sender):
        return copy(
            wsend.at[piece_at(owner)], wrecv.at[sender],
            s_ws.at[owner], r_ws.at[sender], device(owner),
        )

    @pl.loop(0, NOWN)
    def _(owner):
        @pl.when(owner != me)
        def _():
            ws_copy(owner, me).start()

    @pl.when(me < NOWN)
    def _():
        wrecv[me] = wsend[piece_at(me), :]

    RR = 4

    @pl.loop(0, R // RR)
    def _(step):
        i0 = step * RR
        taps = [g3[pl.ds(HALO + i0 - (a - 1) * e2, RR)].reshape(RR * B, 3 * C) for a in range(3)]
        r = dot(taps[0], w2t[0]) + dot(taps[1], w2t[1]) + dot(taps[2], w2t[2])
        r = r.reshape(RR, B, C)
        for k in range(RR):
            gm = g3[HALO + i0 + k, :, C : 2 * C].astype(F32)
            m = mrow[1, HALO : HALO + B, :]
            u = rounded(0.5 * m * (gm + slope[i0 + k] * r[k]))
            rowpart[pl.ds(i0 + k, 1), :] = jnp.sum(u, axis=0, keepdims=True)
            colpart[pl.ds(i0 + k, B), :] += u

    PARTS = RATIO + 1

    def g_move(source, slot, target, quarter, index, action):
        dev_is_me = (target == s) & (quarter == d)

        @pl.when((target < S) & jnp.logical_not(dev_is_me))
        def _():
            c = copy(source, gslots.at[slot], s_g.at[index], r_g.at[slot], (target, quarter))
            c.start() if action == "start" else c.wait_send()

        if action == "start":
            @pl.when(dev_is_me)
            def _():
                gslots[slot] = source[...]

    def g_all(action):
        for quarter in range(D):
            g_move(
                rowpart.at[pl.ds(quarter * Q, Q)], d, s, quarter, quarter, action
            )
            for k in range(PARTS):
                g_move(
                    colpart.at[pl.ds(k * R + quarter * Q, Q)],
                    D + d * PARTS + k, s + d * RATIO + k, quarter,
                    D + quarter * PARTS + k, action,
                )

    g_all("start")

    @pl.loop(0, R // RR)
    def _(step):
        i0 = step * RR
        taps = [p3[pl.ds(HALO + i0 + (a - 1) * e2, RR)].reshape(RR * B, 3 * C) for a in range(3)]
        q = dot(taps[0], w2_ref[0].reshape(3 * C, C))
        q = q + dot(taps[1], w2_ref[1].reshape(3 * C, C))
        q = q + dot(taps[2], w2_ref[2].reshape(3 * C, C))
        q = q.reshape(RR, B, C)
        for k in range(RR):
            m = mrow[1, HALO : HALO + B, :]
            out_ref[i0 + k] = (m * (bandin[i0 + k].astype(F32) + q[k])).astype(BF16)

    for diag in range(D):
        @pl.when(d != diag)
        def _():
            copy(gmine, gslots.at[diag], s_g.at[0], r_g.at[diag], (s, diag)).wait_recv()

        for k in range(PARTS):
            slot = D + diag * PARTS + k
            source = s - diag * RATIO - k
            remote = (source >= 0) & jnp.logical_not((source == s) & (d == diag))

            @pl.when(remote)
            def _():
                copy(gmine, gslots.at[slot], s_g.at[0], r_g.at[slot], (source, diag)).wait_recv()

            @pl.when(source < 0)
            def _():
                gslots[slot] = jnp.zeros((Q, C), F32)

    gmine[...] = jnp.sum(gslots[...], axis=0)

    def ga_copy(other, sender):
        return copy(
            gmine, gall.at[pl.ds(pl.multiple_of(sender * Q, Q), Q)],
            s_ga.at[other], r_ga.at[sender], device(other),
        )

    @pl.loop(1, NDEV)
    def _(step):
        ga_copy(lax.rem(me + step, NDEV), me).start()

    gall[pl.ds(pl.multiple_of(me * Q, Q), Q), :] = gmine[...]

    scaling = 1.0 / math.sqrt(N)

    def wa_copy(other, owner):
        return copy(
            wsum, wall.at[piece_at(owner)], s_wa.at[other], r_wa.at[owner], device(other)
        )

    @pl.when(me < NOWN)
    def _():
        @pl.loop(1, NDEV)
        def _(step):
            other = lax.rem(me + step, NDEV)
            ws_copy(me, other).wait_recv()

        total = wrecv[0].astype(F32)
        for k in range(1, NDEV):
            total = total + wrecv[k].astype(F32)
        wsum[...] = (total * scaling).astype(BF16)

        @pl.loop(1, NDEV)
        def _(step):
            wa_copy(lax.rem(me + step, NDEV), me).start()

        wall[piece_at(me), :] = wsum[...]

    @pl.loop(1, NDEV)
    def _(step):
        other = lax.rem(me + step, NDEV)
        ga_copy(other, other).wait_recv()

    for layer in reversed(range(LINE_LAYERS)):
        e = dil_ref[layer]
        for first in range(0, N, CH):
            gpad[HALO + first : HALO + first + CH, :] = rounded(gall[first : first + CH, :])
        for t in range(3):
            total = None
            for first in range(0, N, CH):
                tap = acts[layer, pl.ds(HALO + first + (t - 1) * e, CH), :].astype(BF16)
                gb = gpad[HALO + first : HALO + first + CH, :].astype(BF16)
                term = dot(tap, gb, ((0,), (0,)))
                total = term if total is None else total + term
            c1_ref[layer, t] = total * scaling
        for first in range(0, N, CH):
            total = None
            for t in range(3):
                tap = gpad[pl.ds(HALO + first - (t - 1) * e, CH), :].astype(BF16)
                term = dot(tap, w1_ref[layer, t], ((1,), (1,)))
                total = term if total is None else total + term
            if layer == 0:
                h = feat_all[first : first + CH, :].astype(F32)
            else:
                h = h1[first : first + CH, :]
            gall[first : first + CH, :] += slope_from(h, gelu_pair(h)[1]) * total
    seqg_ref[...] = gall[pl.ds(pl.multiple_of(row0, R), R), :]

    @pl.loop(0, NOWN)
    def _(owner):
        @pl.when(owner != me)
        def _():
            wa_copy(me, owner).wait_recv()

    c2_ref[...] = wall[...].astype(F32)

    @pl.loop(1, S)
    def _(step):
        feat_copy(lax.rem(s + step, S)).wait_send()

    for a, b in neighbours:
        @pl.when(exists(a, b))
        def _():
            mask_copy(a, b).wait_send()
            halo_copy(a, b).wait_send()

    g_all("wait")

    @pl.loop(0, NOWN)
    def _(owner):
        @pl.when(owner != me)
        def _():
            ws_copy(owner, me).wait_send()

    @pl.loop(1, NDEV)
    def _(step):
        other = lax.rem(me + step, NDEV)
        ga_copy(other, me).wait_send()

        @pl.when(me < NOWN)
        def _():
            wa_copy(other, me).wait_send()


def body(seq_feat, conv1_weight, conv2_kernel_weight, dilations, block_mask, band_grad):
    S = lax.axis_size("seq")
    D = lax.axis_size("diag")
    R, C = seq_feat.shape
    B = band_grad.shape[1]
    N = R * S
    W = B * D
    NDEV = S * D
    NOWN = owners_for(9 * C // 16, NDEV)
    PIECE = 9 * C // NOWN
    PARTS = B // R + 1
    Q = R // D
    RH, WIDE = R + 2 * HALO, B + 2 * HALO
    vmem = pl.BlockSpec(memory_space=pltpu.VMEM)
    smem = pl.BlockSpec(memory_space=pltpu.SMEM)
    dma = pltpu.SemaphoreType.DMA
    scratch = [
        pltpu.VMEM((N, C), BF16),
        pltpu.VMEM((HOFF + N + W + 32, C), F32),
        pltpu.VMEM((N, C), F32),
        pltpu.VMEM((LINE_LAYERS, N + 2 * HALO, C), F32),
        pltpu.VMEM((3, 3, 16, C), F32),
        pltpu.VMEM((3, WIDE, C), F32),
        pltpu.VMEM((RH, WIDE, C), F32),
        pltpu.VMEM((RH, B, 3 * C), BF16),
        pltpu.VMEM((RH, B, 3 * C), BF16),
        pltpu.VMEM((R, B, C), F32),
        pltpu.VMEM((R, B, C), BF16),
        pltpu.VMEM((3, 3 * C, C), BF16),
        pltpu.VMEM((HALO, B, C), BF16),
        pltpu.VMEM((HALO, B, C), BF16),
        pltpu.VMEM((R, 16, C), BF16),
        pltpu.VMEM((R, 16, C), BF16),
        pltpu.VMEM((2, 2, HALO, 16, C), BF16),
        pltpu.VMEM((3, C, 3 * C), F32),
        pltpu.VMEM((9 * C, C), BF16),
        pltpu.VMEM((NDEV, PIECE, C), BF16),
        pltpu.VMEM((PIECE, C), BF16),
        pltpu.VMEM((9 * C, C), BF16),
        pltpu.VMEM((R, C), F32),
        pltpu.VMEM((R + B, C), F32),
        pltpu.VMEM((D + D * PARTS, Q, C), F32),
        pltpu.VMEM((Q, C), F32),
        pltpu.VMEM((N, C), F32),
        pltpu.VMEM((N + 2 * HALO, C), F32),
        dma((S,)), dma((S,)),
        dma((3, 3)), dma((3, 3)),
        dma((3, 3)), dma((3, 3)),
        dma((NDEV,)), dma((NDEV,)),
        dma((NDEV,)), dma((NDEV,)),
        dma((D + D * PARTS,)), dma((D + D * PARTS,)),
        dma((NDEV,)), dma((NDEV,)),
    ]
    band_out, seq_grad, conv1_grad, conv2_grad = pl.pallas_call(
        functools.partial(kernel, S, D, R, B, C, NOWN),
        out_shape=(
            jax.ShapeDtypeStruct((R, B, C), BF16),
            jax.ShapeDtypeStruct((R, C), F32),
            jax.ShapeDtypeStruct((LINE_LAYERS, 3, C, C), F32),
            jax.ShapeDtypeStruct((9 * C, C), F32),
        ),
        in_specs=[vmem, vmem, vmem, smem, smem, vmem],
        out_specs=(vmem, vmem, vmem, vmem),
        scratch_shapes=scratch,
        compiler_params=pltpu.CompilerParams(
            collective_id=0, has_side_effects=True, vmem_limit_bytes=58 * 1024 * 1024
        ),
        name="section",
    )(seq_feat, conv1_weight, conv2_kernel_weight, dilations, block_mask, band_grad)
    return band_out, seq_grad, conv1_grad, conv2_grad.reshape(3, 3, C, C)


def solution(mesh):
    return jax.shard_map(
        body,
        mesh=mesh,
        in_specs=(P("seq", None), P(), P(), P(), P("seq", "diag"), P("seq", "diag", None)),
        out_specs=(P("seq", "diag", None), P("seq", None), P(), P()),
        check_vma=False,
    )
```

profile of v0, /device:TPU:25, one launch (start us, length us, event | category | flops | bytes accessed | tf_op | source)
XLA Modules:
  0.0 74.0 jit_solution(6241266165272612838)
XLA Ops:
  0.6 67.9 %section.1 = (bf16[64,128,128]{2,1,0:T(8,128)(2,1)}, f32[64,128]{1,0:T(8,128)}, f32[2,3,128,128]{3,2,1,0:T(8,128)}, f32[1152,128]{1,0:T(8,128)}) custom-call(bf16[64,128]{1,0:T(8,128)(2,1)} %feat_ref.1, bf16[2,3,128,128]{3,2,1,0:T(8,128)(2,1)} %w1_ref.1, bf16[3,3,128,128]{3,2,1,0:T(8,128)(2,1)} %w2_ref.1, s32[3]{0:T(128)} %dil_ref.1, s32[1,2]{1,0:T(1,128)} %mask_ref.1, ...), custom_call_target="tpu_custom_call" | custom-call | tf_op jit(solution)/shard_map/section/pallas_call | solution.py:526
  68.6 0.0 copy-start.2
  68.6 0.0 copy-start.1
  68.6 0.0 copy-start
  68.6 3.2 %copy.14 = bf16[64,128,128]{2,1,0:T(8,128)(2,1)} copy(bf16[64,128,128]{2,1,0:T(8,128)(2,1)} %get-tuple-element.16) | data formatting | bytes 4194304
  71.8 0.0 copy-done.2
  71.8 0.6 copy.15
  72.5 0.0 copy-done.1
  72.5 0.7 %copy.16 = f32[2,3,128,128]{3,2,1,0:T(8,128)} copy(f32[2,3,128,128]{3,2,1,0:T(8,128)S(1)} %copy-done.1) | data formatting | bytes 786432
  73.2 0.0 copy-done
  73.2 0.8 %copy.17 = f32[3,3,128,128]{3,2,1,0:T(8,128)} copy(f32[3,3,128,128]{3,2,1,0:T(8,128)S(1)} %bitcast.1) | data formatting | bytes 1179648
Async XLA Ops:
  68.6 3.3 %copy-start.2 = (f32[64,128]{1,0:T(8,128)S(1)}, f32[64,128]{1,0:T(8,128)}, u32[]{:S(2)}) copy-start(f32[64,128]{1,0:T(8,128)} %get-tuple-element.17) | copy-start | bytes 98308
  68.6 3.9 %copy-start.1 = (f32[2,3,128,128]{3,2,1,0:T(8,128)S(1)}, f32[2,3,128,128]{3,2,1,0:T(8,128)}, u32[]{:S(2)}) copy-start(f32[2,3,128,128]{3,2,1,0:T(8,128)} %get-tuple-element.18) | copy-start | bytes 1179652
  68.6 4.6 %copy-start = (f32[1152,128]{1,0:T(8,128)S(1)}, f32[1152,128]{1,0:T(8,128)}, u32[]{:S(2)}) copy-start(f32[1152,128]{1,0:T(8,128)} %get-tuple-element.11) | copy-start | bytes 1769476
where the time goes:
time: 74.2 us; the launch traced here: 74 us
  Pallas kernels  67.9 us (92%)
  local copies, waits for them, and re-layouts  5.43 us (7%)
    pallas_call x1, Pallas kernels, body(): pl.pallas_call(functools.partial(kernel, S, D, R, B, C, NOWN), out_shape=...  67.9 us
    unnamed x10, local copies, waits for them, and re-layouts  5.43 us

commit v1 on v0

--- a/solution.py
+++ b/solution.py
@@ -48,9 +48,9 @@
     out_ref, seqg_ref, c1_ref, c2_ref,
     feat_all, hid, h1, acts, maskt, mrow, wide, p3, g3, slope, bandin, w2t,
     top, bottom, left, right, corner,
-    wg, wsend, wrecv, wsum, wall, rowpart, colpart, gslots, gmine, gall, gpad,
+    wg, wsend, wrecv, wsum, wall, rowpart, colpart, gslots, gmine, gall, gpad, gallb, out_scr,
     s_feat, r_feat, s_halo, r_halo, s_mask, r_mask, s_ws, r_ws, s_wa, r_wa,
-    s_g, r_g, s_ga, r_ga,
+    s_g, r_g, s_ga, r_ga, s_out,
 ):
     N = R * S
     W = B * D
@@ -129,7 +129,9 @@
         def _():
             mask_copy(a, b).start()
 
-    for a, b in neighbours:
+    sides = [(0, -1), (0, 1)]
+    edges = [(-1, 0), (1, 0), (-1, -1), (-1, 1), (1, -1), (1, 1)]
+    for a, b in sides + edges:
         @pl.when(exists(a, b))
         def _():
             halo_copy(a, b).start()
@@ -233,13 +235,16 @@
         wide[li] = rounded(gelu_pair(band_row(li, 2 * (1 - low)))[0])
         spread(p3, li, 1)
 
-    for a, b in neighbours:
-        @pl.when(exists(a, b))
-        def _():
-            copy(
-                halo_slot(a, b), halo_slot(a, b),
-                s_halo.at[1 + a, 1 + b], r_halo.at[1 + a, 1 + b], (s + a, d + b),
-            ).wait_recv()
+    def wait_halos(which):
+        for a, b in which:
+            @pl.when(exists(a, b))
+            def _():
+                copy(
+                    halo_slot(a, b), halo_slot(a, b),
+                    s_halo.at[1 + a, 1 + b], r_halo.at[1 + a, 1 + b], (s + a, d + b),
+                ).wait_recv()
+
+    wait_halos(sides)
 
     def gm_row(li, kind, lo, mid, hi):
         wide[li, 0:HALO, :] = mrow[kind, 0:HALO, :] * lo.astype(F32)[8:16]
@@ -251,11 +256,6 @@
     def _(i):
         gm_row(i + HALO, 1, left[i], grad_ref[i], right[i])
 
-    @pl.loop(0, HALO)
-    def _(i):
-        gm_row(i, 0, corner[0, 0, i], top[i], corner[0, 1, i])
-        gm_row(i + HALO + R, 2, corner[1, 0, i], bottom[i], corner[1, 1, i])
-
     KR = 8
 
     @pl.loop(0, R // KR)
@@ -293,8 +293,7 @@
 
     RR = 4
 
-    @pl.loop(0, R // RR)
-    def _(step):
+    def back_rows(step):
         i0 = step * RR
         taps = [g3[pl.ds(HALO + i0 - (a - 1) * e2, RR)].reshape(RR * B, 3 * C) for a in range(3)]
         r = dot(taps[0], w2t[0]) + dot(taps[1], w2t[1]) + dot(taps[2], w2t[2])
@@ -305,6 +304,17 @@
             u = rounded(0.5 * m * (gm + slope[i0 + k] * r[k]))
             rowpart[pl.ds(i0 + k, 1), :] = jnp.sum(u, axis=0, keepdims=True)
             colpart[pl.ds(i0 + k, B), :] += u
+
+    pl.loop(HALO // RR, (R - HALO) // RR)(back_rows)
+    wait_halos(edges)
+
+    @pl.loop(0, HALO)
+    def _(i):
+        gm_row(i, 0, corner[0, 0, i], top[i], corner[0, 1, i])
+        gm_row(i + HALO + R, 2, corner[1, 0, i], bottom[i], corner[1, 1, i])
+
+    pl.loop(0, HALO // RR)(back_rows)
+    pl.loop((R - HALO) // RR, R // RR)(back_rows)
 
     PARTS = RATIO + 1
 
@@ -345,12 +355,15 @@
         q = q.reshape(RR, B, C)
         for k in range(RR):
             m = mrow[1, HALO : HALO + B, :]
-            out_ref[i0 + k] = (m * (bandin[i0 + k].astype(F32) + q[k])).astype(BF16)
+            out_scr[i0 + k] = (m * (bandin[i0 + k].astype(F32) + q[k])).astype(BF16)
+
+    out_copy = pltpu.make_async_copy(out_scr, out_ref, s_out)
+    out_copy.start()
 
     for diag in range(D):
         @pl.when(d != diag)
         def _():
-            copy(gmine, gslots.at[diag], s_g.at[0], r_g.at[diag], (s, diag)).wait_recv()
+            copy(rowpart.at[pl.ds(0, Q)], gslots.at[diag], s_g.at[0], r_g.at[diag], (s, diag)).wait_recv()
 
         for k in range(PARTS):
             slot = D + diag * PARTS + k
@@ -359,17 +372,17 @@
 
             @pl.when(remote)
             def _():
-                copy(gmine, gslots.at[slot], s_g.at[0], r_g.at[slot], (source, diag)).wait_recv()
+                copy(rowpart.at[pl.ds(0, Q)], gslots.at[slot], s_g.at[0], r_g.at[slot], (source, diag)).wait_recv()
 
             @pl.when(source < 0)
             def _():
                 gslots[slot] = jnp.zeros((Q, C), F32)
 
-    gmine[...] = jnp.sum(gslots[...], axis=0)
+    gmine[...] = jnp.sum(gslots[...], axis=0).astype(BF16)
 
     def ga_copy(other, sender):
         return copy(
-            gmine, gall.at[pl.ds(pl.multiple_of(sender * Q, Q), Q)],
+            gmine, gallb.at[pl.ds(pl.multiple_of(sender * Q, Q), Q)],
             s_ga.at[other], r_ga.at[sender], device(other),
         )
 
@@ -377,7 +390,7 @@
     def _(step):
         ga_copy(lax.rem(me + step, NDEV), me).start()
 
-    gall[pl.ds(pl.multiple_of(me * Q, Q), Q), :] = gmine[...]
+    gallb[pl.ds(pl.multiple_of(me * Q, Q), Q), :] = gmine[...]
 
     scaling = 1.0 / math.sqrt(N)
 
@@ -408,6 +421,8 @@
     def _(step):
         other = lax.rem(me + step, NDEV)
         ga_copy(other, other).wait_recv()
+
+    gall[...] = gallb[...].astype(F32)
 
     for layer in reversed(range(LINE_LAYERS)):
         e = dil_ref[layer]
@@ -442,6 +457,8 @@
 
     c2_ref[...] = wall[...].astype(F32)
 
+    out_copy.wait()
+
     @pl.loop(1, S)
     def _(step):
         feat_copy(lax.rem(s + step, S)).wait_send()
@@ -468,6 +485,23 @@
         @pl.when(me < NOWN)
         def _():
             wa_copy(other, me).wait_send()
+
+
+def place(parts, *refs):
+    count = len(parts)
+    sources, targets, sems = refs[:count], refs[count : 2 * count], refs[2 * count]
+    copies = []
+    for source, target, pieces in zip(sources, targets, parts):
+        size = source.shape[0] // pieces
+        for k in range(pieces):
+            rows = pl.ds(k * size, size)
+            copies.append(
+                pltpu.make_async_copy(source.at[rows], target.at[rows], sems.at[len(copies)])
+            )
+    for c in copies:
+        c.start()
+    for c in copies:
+        c.wait()
 
 
 def body(seq_feat, conv1_weight, conv2_kernel_weight, dilations, block_mask, band_grad):
@@ -512,16 +546,18 @@
         pltpu.VMEM((R, C), F32),
         pltpu.VMEM((R + B, C), F32),
         pltpu.VMEM((D + D * PARTS, Q, C), F32),
-        pltpu.VMEM((Q, C), F32),
+        pltpu.VMEM((Q, C), BF16),
         pltpu.VMEM((N, C), F32),
         pltpu.VMEM((N + 2 * HALO, C), F32),
+        pltpu.VMEM((N, C), BF16),
+        pltpu.VMEM((R, B, C), BF16),
         dma((S,)), dma((S,)),
         dma((3, 3)), dma((3, 3)),
         dma((3, 3)), dma((3, 3)),
         dma((NDEV,)), dma((NDEV,)),
         dma((NDEV,)), dma((NDEV,)),
         dma((D + D * PARTS,)), dma((D + D * PARTS,)),
-        dma((NDEV,)), dma((NDEV,)),
+        dma((NDEV,)), dma((NDEV,)), dma,
     ]
     band_out, seq_grad, conv1_grad, conv2_grad = pl.pallas_call(
         functools.partial(kernel, S, D, R, B, C, NOWN),
@@ -532,13 +568,25 @@
             jax.ShapeDtypeStruct((9 * C, C), F32),
         ),
         in_specs=[vmem, vmem, vmem, smem, smem, vmem],
-        out_specs=(vmem, vmem, vmem, vmem),
+        out_specs=(pl.BlockSpec(memory_space=pl.ANY), vmem, vmem, vmem),
         scratch_shapes=scratch,
         compiler_params=pltpu.CompilerParams(
-            collective_id=0, has_side_effects=True, vmem_limit_bytes=58 * 1024 * 1024
+            collective_id=0, has_side_effects=True, vmem_limit_bytes=min(58 << 20, (48 << 20) + 28 * N * C)
         ),
         name="section",
     )(seq_feat, conv1_weight, conv2_kernel_weight, dilations, block_mask, band_grad)
+    results = (band_out, seq_grad, conv1_grad, conv2_grad)
+    parts = (8, 1, 2, 3)
+    anywhere = pl.BlockSpec(memory_space=pl.ANY)
+    band_out, seq_grad, conv1_grad, conv2_grad = pl.pallas_call(
+        functools.partial(place, parts),
+        out_shape=tuple(jax.ShapeDtypeStruct(x.shape, x.dtype) for x in results),
+        in_specs=[anywhere] * 4,
+        out_specs=(anywhere,) * 4,
+        scratch_shapes=[dma((sum(parts),))],
+        compiler_params=pltpu.CompilerParams(vmem_limit_bytes=1024 * 1024),
+        name="place",
+    )(*results)
     return band_out, seq_grad, conv1_grad, conv2_grad.reshape(3, 3, C, C)
 
 

time: 74.2 us -> 62.9 us (0.85)
  Pallas kernels: 67.9 us -> 57.9 us
  local copies, waits for them, and re-layouts: 5.43 us -> 3.91 us
    pallas_call x1, Pallas kernels: 67.9 us -> 56.1 us  [body(): pl.pallas_call(functools.partial(kernel, S, D, R, B, C, NOWN), out_shape=...]
    pallas_call x0 -> x1, Pallas kernels: none -> 1.76 us  [body(): pl.pallas_call(functools.partial(place, parts), out_shape=tuple((jax.Shap...]
    unnamed x10, local copies, waits for them, and re-layouts: 5.43 us -> 3.91 us
where the time goes in v1:
time: 62.9 us; the launch traced here: 62.4 us
  Pallas kernels  57.9 us (92%)
  local copies, waits for them, and re-layouts  3.91 us (6%)
  between operations  0.65 us (1%)
    pallas_call x1, Pallas kernels, body(): pl.pallas_call(functools.partial(kernel, S, D, R, B, C, NOWN), out_shape=...  56.1 us
    unnamed x10, local copies, waits for them, and re-layouts  3.91 us
    pallas_call x1, Pallas kernels, body(): pl.pallas_call(functools.partial(place, parts), out_shape=tuple((jax.Shap...  1.76 us

profile of v1, /device:TPU:25, one launch (start us, length us, event | category | flops | bytes accessed | tf_op | source)
XLA Modules:
  0.0 62.4 jit_solution(8917374601829103437)
XLA Ops:
  0.6 0.0 copy-start
  0.6 1.0 %copy-done = bf16[3,3,128,128]{3,2,1,0:T(8,128)(2,1)S(1)} copy-done((bf16[3,3,128,128]{3,2,1,0:T(8,128)(2,1)S(1)}, bf16[3,3,128,128]{3,2,1,0:T(8,128)(2,1)}, u32[]{:S(2)}) %copy-start) | copy-done | bytes 294936
  1.6 0.0 copy-start.1
  1.6 0.9 %copy-done.1 = bf16[2,3,128,128]{3,2,1,0:T(8,128)(2,1)S(1)} copy-done((bf16[2,3,128,128]{3,2,1,0:T(8,128)(2,1)S(1)}, bf16[2,3,128,128]{3,2,1,0:T(8,128)(2,1)}, u32[]{:S(2)}) %copy-start.1) | copy-done | bytes 196632
  2.5 0.0 copy-start.2
  2.5 0.7 %copy-done.2 = bf16[64,128]{1,0:T(8,128)(2,1)S(1)} copy-done((bf16[64,128]{1,0:T(8,128)(2,1)S(1)}, bf16[64,128]{1,0:T(8,128)(2,1)}, u32[]{:S(2)}) %copy-start.2) | copy-done | bytes 16408
  3.2 0.0 copy-start.3
  3.2 0.7 %copy-done.3 = s32[3]{0:T(128)S(1)} copy-done((s32[3]{0:T(128)S(1)}, s32[3]{0:T(128)}, u32[]{:S(2)}) %copy-start.3) | copy-done | bytes 36
  3.9 0.0 copy-start.4
  3.9 0.7 %copy-done.4 = s32[1,2]{1,0:T(1,128)S(1)} copy-done((s32[1,2]{1,0:T(1,128)S(1)}, s32[1,2]{1,0:T(1,128)}, u32[]{:S(2)}) %copy-start.4) | copy-done | bytes 32
  4.6 56.1 %section.1 = (bf16[64,128,128]{2,1,0:T(8,128)(2,1)S(1)}, f32[64,128]{1,0:T(8,128)S(1)}, f32[2,3,128,128]{3,2,1,0:T(8,128)S(1)}, f32[1152,128]{1,0:T(8,128)S(1)}) custom-call(bf16[64,128]{1,0:T(8,128)(2,1)S(1)} %copy-done.2, bf16[2,3,128,128]{3,2,1,0:T(8,128)(2,1)S(1)} %copy-done.1, bf16[3,3,128,128]{3,2,1,0:T(8,128)(2,1)S(1)} %copy-done, s32[3]{0:T(128)S(1)} %copy-done.3, ...), custom_call_target="tpu_custom_call" | custom-call | tf_op jit(solution)/shard_map/section/pallas_call | solution.py:562
  60.7 1.8 %place.1 = (bf16[64,128,128]{2,1,0:T(8,128)(2,1)}, f32[64,128]{1,0:T(8,128)}, f32[2,3,128,128]{3,2,1,0:T(8,128)}, f32[1152,128]{1,0:T(8,128)}) custom-call(bf16[64,128,128]{2,1,0:T(8,128)(2,1)S(1)} %get-tuple-element.12.refs_0_, f32[64,128]{1,0:T(8,128)S(1)} %get-tuple-element.13.refs_1_, f32[2,3,128,128]{3,2,1,0:T(8,128)S(1)} %get-tuple-element.14.refs_2_, ...), custom_call_target="tpu_custom_call" | custom-call | tf_op jit(solution)/shard_map/place/pallas_call | solution.py:581
Async XLA Ops:
  0.6 1.0 %copy-start = (bf16[3,3,128,128]{3,2,1,0:T(8,128)(2,1)S(1)}, bf16[3,3,128,128]{3,2,1,0:T(8,128)(2,1)}, u32[]{:S(2)}) copy-start(bf16[3,3,128,128]{3,2,1,0:T(8,128)(2,1)} %w2_ref.1) | copy-start | bytes 884740
  1.6 0.9 %copy-start.1 = (bf16[2,3,128,128]{3,2,1,0:T(8,128)(2,1)S(1)}, bf16[2,3,128,128]{3,2,1,0:T(8,128)(2,1)}, u32[]{:S(2)}) copy-start(bf16[2,3,128,128]{3,2,1,0:T(8,128)(2,1)} %w1_ref.1) | copy-start | bytes 589828
  2.5 0.7 %copy-start.2 = (bf16[64,128]{1,0:T(8,128)(2,1)S(1)}, bf16[64,128]{1,0:T(8,128)(2,1)}, u32[]{:S(2)}) copy-start(bf16[64,128]{1,0:T(8,128)(2,1)} %feat_ref.1) | copy-start | bytes 49156
  3.2 0.7 %copy-start.3 = (s32[3]{0:T(128)S(1)}, s32[3]{0:T(128)}, u32[]{:S(2)}) copy-start(s32[3]{0:T(128)} %dil_ref.1) | copy-start | bytes 40
  3.9 0.7 %copy-start.4 = (s32[1,2]{1,0:T(1,128)S(1)}, s32[1,2]{1,0:T(1,128)}, u32[]{:S(2)}) copy-start(s32[1,2]{1,0:T(1,128)} %mask_ref.1) | copy-start | bytes 28

commit v2 on v1

--- a/solution.py
+++ b/solution.py
@@ -44,11 +44,12 @@
 
 def kernel(
     S, D, R, B, C, NOWN,
-    feat_ref, w1_ref, w2_ref, dil_ref, mask_ref, grad_ref,
+    feat_ref, w1_hbm, w2_hbm, dil_hbm, mask_hbm, grad_hbm,
     out_ref, seqg_ref, c1_ref, c2_ref,
     feat_all, hid, h1, acts, maskt, mrow, wide, p3, g3, slope, bandin, w2t,
     top, bottom, left, right, corner,
     wg, wsend, wrecv, wsum, wall, rowpart, colpart, gslots, gmine, gall, gpad, gallb, out_scr,
+    w1_ref, w2_ref, dil_ref, mask_ref, grad_ref, s_in,
     s_feat, r_feat, s_halo, r_halo, s_mask, r_mask, s_ws, r_ws, s_wa, r_wa,
     s_g, r_g, s_ga, r_ga, s_out,
 ):
@@ -63,7 +64,6 @@
     me = s * D + d
     row0 = s * R
     d0 = d * B
-    e2 = dil_ref[LINE_LAYERS]
 
     def device(index):
         return (index // D, index % D)
@@ -74,6 +74,22 @@
             device_id=dev, device_id_type=MESH,
         )
 
+    own_rows = feat_all.at[pl.ds(pl.multiple_of(row0, R), R)]
+    loads = [
+        pltpu.make_async_copy(source, target, s_in.at[k])
+        for k, (source, target) in enumerate(
+            [
+                (mask_hbm, mask_ref), (dil_hbm, dil_ref), (feat_ref, own_rows),
+                (w1_hbm, w1_ref), (w2_hbm, w2_ref), (grad_hbm, grad_ref),
+            ]
+        )
+    ]
+    for load in loads:
+        load.start()
+
+    loads[0].wait()
+    loads[1].wait()
+    e2 = dil_ref[LINE_LAYERS]
     for k in range(2):
         value = mask_ref[0, k].astype(F32)
         maskt[1, 1, 8 * k : 8 * k + 8, :] = jnp.full((8, C), 1.0, F32) * value
@@ -120,7 +136,7 @@
         rows = {-1: pl.ds(0, HALO), 0: pl.ds(0, R), 1: pl.ds(R - HALO, HALO)}[a]
         cols = {-1: pl.ds(0, 16), 0: pl.ds(0, B), 1: pl.ds(B - 16, 16)}[b]
         return copy(
-            grad_ref.at[rows, cols], halo_slot(-a, -b),
+            grad_hbm.at[rows, cols], halo_slot(-a, -b),
             s_halo.at[1 + a, 1 + b], r_halo.at[1 - a, 1 - b], (s + a, d + b),
         )
 
@@ -142,7 +158,8 @@
             slot = halo_slot(a, b)
             slot[...] = jnp.zeros(slot.shape, BF16)
 
-    feat_all[pl.ds(pl.multiple_of(row0, R), R), :] = feat_ref[...]
+    for load in loads[2:]:
+        load.wait()
     hid[0:HOFF, :] = jnp.zeros((HOFF, C), F32)
     hid[HOFF + N :, :] = jnp.zeros((hid.shape[0] - HOFF - N, C), F32)
     for layer in range(LINE_LAYERS):
@@ -345,6 +362,31 @@
 
     g_all("start")
 
+    scaling = 1.0 / math.sqrt(N)
+
+    def wa_copy(other, owner):
+        return copy(
+            wsum, wall.at[piece_at(owner)], s_wa.at[other], r_wa.at[owner], device(other)
+        )
+
+    @pl.when(me < NOWN)
+    def _():
+        @pl.loop(1, NDEV)
+        def _(step):
+            other = lax.rem(me + step, NDEV)
+            ws_copy(me, other).wait_recv()
+
+        total = wrecv[0].astype(F32)
+        for k in range(1, NDEV):
+            total = total + wrecv[k].astype(F32)
+        wsum[...] = (total * scaling).astype(BF16)
+
+        @pl.loop(1, NDEV)
+        def _(step):
+            wa_copy(lax.rem(me + step, NDEV), me).start()
+
+        wall[piece_at(me), :] = wsum[...]
+
     @pl.loop(0, R // RR)
     def _(step):
         i0 = step * RR
@@ -391,31 +433,6 @@
         ga_copy(lax.rem(me + step, NDEV), me).start()
 
     gallb[pl.ds(pl.multiple_of(me * Q, Q), Q), :] = gmine[...]
-
-    scaling = 1.0 / math.sqrt(N)
-
-    def wa_copy(other, owner):
-        return copy(
-            wsum, wall.at[piece_at(owner)], s_wa.at[other], r_wa.at[owner], device(other)
-        )
-
-    @pl.when(me < NOWN)
-    def _():
-        @pl.loop(1, NDEV)
-        def _(step):
-            other = lax.rem(me + step, NDEV)
-            ws_copy(me, other).wait_recv()
-
-        total = wrecv[0].astype(F32)
-        for k in range(1, NDEV):
-            total = total + wrecv[k].astype(F32)
-        wsum[...] = (total * scaling).astype(BF16)
-
-        @pl.loop(1, NDEV)
-        def _(step):
-            wa_copy(lax.rem(me + step, NDEV), me).start()
-
-        wall[piece_at(me), :] = wsum[...]
 
     @pl.loop(1, NDEV)
     def _(step):
@@ -518,7 +535,6 @@
     Q = R // D
     RH, WIDE = R + 2 * HALO, B + 2 * HALO
     vmem = pl.BlockSpec(memory_space=pltpu.VMEM)
-    smem = pl.BlockSpec(memory_space=pltpu.SMEM)
     dma = pltpu.SemaphoreType.DMA
     scratch = [
         pltpu.VMEM((N, C), BF16),
@@ -551,6 +567,12 @@
         pltpu.VMEM((N + 2 * HALO, C), F32),
         pltpu.VMEM((N, C), BF16),
         pltpu.VMEM((R, B, C), BF16),
+        pltpu.VMEM(conv1_weight.shape, BF16),
+        pltpu.VMEM(conv2_kernel_weight.shape, BF16),
+        pltpu.SMEM(dilations.shape, jnp.int32),
+        pltpu.SMEM(block_mask.shape, jnp.int32),
+        pltpu.VMEM((R, B, C), BF16),
+        dma((6,)),
         dma((S,)), dma((S,)),
         dma((3, 3)), dma((3, 3)),
         dma((3, 3)), dma((3, 3)),
@@ -567,7 +589,7 @@
             jax.ShapeDtypeStruct((LINE_LAYERS, 3, C, C), F32),
             jax.ShapeDtypeStruct((9 * C, C), F32),
         ),
-        in_specs=[vmem, vmem, vmem, smem, smem, vmem],
+        in_specs=[pl.BlockSpec(memory_space=pltpu.HBM)] * 6,
         out_specs=(pl.BlockSpec(memory_space=pl.ANY), vmem, vmem, vmem),
         scratch_shapes=scratch,
         compiler_params=pltpu.CompilerParams(

time: 62.9 us -> 59.7 us (0.949)
  the two profiles are of different devices: /device:TPU:25 before, /device:TPU:0 now
where the time goes in v2:
time: 59.7 us; the launch traced here: 59.4 us
  Pallas kernels  54.9 us (92%)
  local copies, waits for them, and re-layouts  3.91 us (7%)
  between operations  0.65 us (1%)
    pallas_call x1, Pallas kernels, body(): pl.pallas_call(functools.partial(kernel, S, D, R, B, C, NOWN), out_shape=...  53.1 us
    unnamed x10, local copies, waits for them, and re-layouts  3.91 us
    pallas_call x1, Pallas kernels, body(): pl.pallas_call(functools.partial(place, parts), out_shape=tuple((jax.Shap...  1.76 us

profile of v2, /device:TPU:0, one launch (start us, length us, event | category | flops | bytes accessed | tf_op | source)
XLA Modules:
  0.0 59.4 jit_solution(3996610734955549546)
XLA Ops:
  0.6 0.0 copy-start
  0.6 1.0 %copy-done = bf16[3,3,128,128]{3,2,1,0:T(8,128)(2,1)S(1)} copy-done((bf16[3,3,128,128]{3,2,1,0:T(8,128)(2,1)S(1)}, bf16[3,3,128,128]{3,2,1,0:T(8,128)(2,1)}, u32[]{:S(2)}) %copy-start) | copy-done | bytes 294936
  1.6 0.0 copy-start.1
  1.6 0.9 %copy-done.1 = bf16[2,3,128,128]{3,2,1,0:T(8,128)(2,1)S(1)} copy-done((bf16[2,3,128,128]{3,2,1,0:T(8,128)(2,1)S(1)}, bf16[2,3,128,128]{3,2,1,0:T(8,128)(2,1)}, u32[]{:S(2)}) %copy-start.1) | copy-done | bytes 196632
  2.5 0.0 copy-start.2
  2.5 0.7 %copy-done.2 = bf16[64,128]{1,0:T(8,128)(2,1)S(1)} copy-done((bf16[64,128]{1,0:T(8,128)(2,1)S(1)}, bf16[64,128]{1,0:T(8,128)(2,1)}, u32[]{:S(2)}) %copy-start.2) | copy-done | bytes 16408
  3.2 0.0 copy-start.3
  3.2 0.7 %copy-done.3 = s32[3]{0:T(128)S(1)} copy-done((s32[3]{0:T(128)S(1)}, s32[3]{0:T(128)}, u32[]{:S(2)}) %copy-start.3) | copy-done | bytes 36
  3.9 0.0 copy-start.4
  3.9 0.7 %copy-done.4 = s32[1,2]{1,0:T(1,128)S(1)} copy-done((s32[1,2]{1,0:T(1,128)S(1)}, s32[1,2]{1,0:T(1,128)}, u32[]{:S(2)}) %copy-start.4) | copy-done | bytes 32
  4.6 53.1 %section.1 = (bf16[64,128,128]{2,1,0:T(8,128)(2,1)S(1)}, f32[64,128]{1,0:T(8,128)S(1)}, f32[2,3,128,128]{3,2,1,0:T(8,128)S(1)}, f32[1152,128]{1,0:T(8,128)S(1)}) custom-call(bf16[64,128]{1,0:T(8,128)(2,1)S(1)} %copy-done.2, bf16[2,3,128,128]{3,2,1,0:T(8,128)(2,1)S(1)} %copy-done.1, bf16[3,3,128,128]{3,2,1,0:T(8,128)(2,1)S(1)} %copy-done, s32[3]{0:T(128)S(1)} %copy-done.3, ...), custom_call_target="tpu_custom_call" | custom-call | tf_op jit(solution)/shard_map/section/pallas_call | solution.py:584
  57.7 1.8 %place.1 = (bf16[64,128,128]{2,1,0:T(8,128)(2,1)}, f32[64,128]{1,0:T(8,128)}, f32[2,3,128,128]{3,2,1,0:T(8,128)}, f32[1152,128]{1,0:T(8,128)}) custom-call(bf16[64,128,128]{2,1,0:T(8,128)(2,1)S(1)} %get-tuple-element.12.refs_0_, f32[64,128]{1,0:T(8,128)S(1)} %get-tuple-element.13.refs_1_, f32[2,3,128,128]{3,2,1,0:T(8,128)S(1)} %get-tuple-element.14.refs_2_, ...), custom_call_target="tpu_custom_call" | custom-call | tf_op jit(solution)/shard_map/place/pallas_call | solution.py:603
Async XLA Ops:
  0.6 1.0 %copy-start = (bf16[3,3,128,128]{3,2,1,0:T(8,128)(2,1)S(1)}, bf16[3,3,128,128]{3,2,1,0:T(8,128)(2,1)}, u32[]{:S(2)}) copy-start(bf16[3,3,128,128]{3,2,1,0:T(8,128)(2,1)} %w2_hbm.1) | copy-start | bytes 884740
  1.6 0.9 %copy-start.1 = (bf16[2,3,128,128]{3,2,1,0:T(8,128)(2,1)S(1)}, bf16[2,3,128,128]{3,2,1,0:T(8,128)(2,1)}, u32[]{:S(2)}) copy-start(bf16[2,3,128,128]{3,2,1,0:T(8,128)(2,1)} %w1_hbm.1) | copy-start | bytes 589828
  2.5 0.7 %copy-start.2 = (bf16[64,128]{1,0:T(8,128)(2,1)S(1)}, bf16[64,128]{1,0:T(8,128)(2,1)}, u32[]{:S(2)}) copy-start(bf16[64,128]{1,0:T(8,128)(2,1)} %feat_ref.1) | copy-start | bytes 49156
  3.2 0.7 %copy-start.3 = (s32[3]{0:T(128)S(1)}, s32[3]{0:T(128)}, u32[]{:S(2)}) copy-start(s32[3]{0:T(128)} %dil_hbm.1) | copy-start | bytes 40
  3.9 0.7 %copy-start.4 = (s32[1,2]{1,0:T(1,128)S(1)}, s32[1,2]{1,0:T(1,128)}, u32[]{:S(2)}) copy-start(s32[1,2]{1,0:T(1,128)} %mask_hbm.1) | copy-start | bytes 28

commit v3 on v2

--- a/solution.py
+++ b/solution.py
@@ -308,7 +308,7 @@
     def _():
         wrecv[me] = wsend[piece_at(me), :]
 
-    RR = 4
+    RR = 8
 
     def back_rows(step):
         i0 = step * RR

time: 59.7 us -> 58.5 us (0.980)
  the two profiles are of different devices: /device:TPU:0 before, /device:TPU:25 now
where the time goes in v3:
time: 58.5 us; the launch traced here: 58.3 us
  Pallas kernels  53.7 us (92%)
  local copies, waits for them, and re-layouts  3.91 us (7%)
  between operations  0.65 us (1%)
    pallas_call x1, Pallas kernels, body(): pl.pallas_call(functools.partial(kernel, S, D, R, B, C, NOWN), out_shape=...  52 us
    unnamed x10, local copies, waits for them, and re-layouts  3.91 us
    pallas_call x1, Pallas kernels, body(): pl.pallas_call(functools.partial(place, parts), out_shape=tuple((jax.Shap...  1.76 us

profile of v3, /device:TPU:25, one launch (start us, length us, event | category | flops | bytes accessed | tf_op | source)
XLA Modules:
  0.0 58.3 jit_solution(5392755381355375442)
XLA Ops:
  0.6 0.0 copy-start
  0.6 1.0 %copy-done = bf16[3,3,128,128]{3,2,1,0:T(8,128)(2,1)S(1)} copy-done((bf16[3,3,128,128]{3,2,1,0:T(8,128)(2,1)S(1)}, bf16[3,3,128,128]{3,2,1,0:T(8,128)(2,1)}, u32[]{:S(2)}) %copy-start) | copy-done | bytes 294936
  1.6 0.0 copy-start.1
  1.6 0.9 %copy-done.1 = bf16[2,3,128,128]{3,2,1,0:T(8,128)(2,1)S(1)} copy-done((bf16[2,3,128,128]{3,2,1,0:T(8,128)(2,1)S(1)}, bf16[2,3,128,128]{3,2,1,0:T(8,128)(2,1)}, u32[]{:S(2)}) %copy-start.1) | copy-done | bytes 196632
  2.5 0.0 copy-start.2
  2.5 0.7 %copy-done.2 = bf16[64,128]{1,0:T(8,128)(2,1)S(1)} copy-done((bf16[64,128]{1,0:T(8,128)(2,1)S(1)}, bf16[64,128]{1,0:T(8,128)(2,1)}, u32[]{:S(2)}) %copy-start.2) | copy-done | bytes 16408
  3.2 0.0 copy-start.3
  3.2 0.7 %copy-done.3 = s32[3]{0:T(128)S(1)} copy-done((s32[3]{0:T(128)S(1)}, s32[3]{0:T(128)}, u32[]{:S(2)}) %copy-start.3) | copy-done | bytes 36
  3.9 0.0 copy-start.4
  3.9 0.7 %copy-done.4 = s32[1,2]{1,0:T(1,128)S(1)} copy-done((s32[1,2]{1,0:T(1,128)S(1)}, s32[1,2]{1,0:T(1,128)}, u32[]{:S(2)}) %copy-start.4) | copy-done | bytes 32
  4.6 52.0 %section.1 = (bf16[64,128,128]{2,1,0:T(8,128)(2,1)S(1)}, f32[64,128]{1,0:T(8,128)S(1)}, f32[2,3,128,128]{3,2,1,0:T(8,128)S(1)}, f32[1152,128]{1,0:T(8,128)S(1)}) custom-call(bf16[64,128]{1,0:T(8,128)(2,1)S(1)} %copy-done.2, bf16[2,3,128,128]{3,2,1,0:T(8,128)(2,1)S(1)} %copy-done.1, bf16[3,3,128,128]{3,2,1,0:T(8,128)(2,1)S(1)} %copy-done, s32[3]{0:T(128)S(1)} %copy-done.3, ...), custom_call_target="tpu_custom_call" | custom-call | tf_op jit(solution)/shard_map/section/pallas_call | solution.py:584
  56.5 1.8 %place.1 = (bf16[64,128,128]{2,1,0:T(8,128)(2,1)}, f32[64,128]{1,0:T(8,128)}, f32[2,3,128,128]{3,2,1,0:T(8,128)}, f32[1152,128]{1,0:T(8,128)}) custom-call(bf16[64,128,128]{2,1,0:T(8,128)(2,1)S(1)} %get-tuple-element.12.refs_0_, f32[64,128]{1,0:T(8,128)S(1)} %get-tuple-element.13.refs_1_, f32[2,3,128,128]{3,2,1,0:T(8,128)S(1)} %get-tuple-element.14.refs_2_, ...), custom_call_target="tpu_custom_call" | custom-call | tf_op jit(solution)/shard_map/place/pallas_call | solution.py:603
Async XLA Ops:
  0.6 1.0 %copy-start = (bf16[3,3,128,128]{3,2,1,0:T(8,128)(2,1)S(1)}, bf16[3,3,128,128]{3,2,1,0:T(8,128)(2,1)}, u32[]{:S(2)}) copy-start(bf16[3,3,128,128]{3,2,1,0:T(8,128)(2,1)} %w2_hbm.1) | copy-start | bytes 884740
  1.6 0.9 %copy-start.1 = (bf16[2,3,128,128]{3,2,1,0:T(8,128)(2,1)S(1)}, bf16[2,3,128,128]{3,2,1,0:T(8,128)(2,1)}, u32[]{:S(2)}) copy-start(bf16[2,3,128,128]{3,2,1,0:T(8,128)(2,1)} %w1_hbm.1) | copy-start | bytes 589828
  2.5 0.7 %copy-start.2 = (bf16[64,128]{1,0:T(8,128)(2,1)S(1)}, bf16[64,128]{1,0:T(8,128)(2,1)}, u32[]{:S(2)}) copy-start(bf16[64,128]{1,0:T(8,128)(2,1)} %feat_ref.1) | copy-start | bytes 49156
  3.2 0.7 %copy-start.3 = (s32[3]{0:T(128)S(1)}, s32[3]{0:T(128)}, u32[]{:S(2)}) copy-start(s32[3]{0:T(128)} %dil_hbm.1) | copy-start | bytes 40
  3.9 0.7 %copy-start.4 = (s32[1,2]{1,0:T(1,128)S(1)}, s32[1,2]{1,0:T(1,128)}, u32[]{:S(2)}) copy-start(s32[1,2]{1,0:T(1,128)} %mask_hbm.1) | copy-start | bytes 28
